TPU v7x, 32 devices: a whole 2x2x4 slice. The times are simulated.
32 devices in a mesh: fsdp: 4 (over y, x), ctx: 8 (over z, core).
Axes of the slice: x: 2, y: 2, z: 4, core: 2. Of those that a mesh axis runs over, the one named last changes fastest.
Arguments:
- inputs: bfloat16 [4, 2048, 768], P('fsdp', 'ctx'), may hold values from -6 to 6
- positions: int32 [4, 2048], P('fsdp', 'ctx'), may hold values from 0 to 2047, as said below
- in_weight: bfloat16 [768, 2304], P('fsdp'), may hold values from -0.21875 to 0.21875
- in_bias: bfloat16 [2304], P('fsdp'), may hold values from -0.3125 to 0.3125
- out_weight: bfloat16 [768, 768], P('fsdp'), may hold values from -0.109375 to 0.109375
- out_bias: bfloat16 [768], P('fsdp'), may hold values from -4 to 4
- up_weight: bfloat16 [768, 3072], P('fsdp'), may hold values from -0.21875 to 0.21875
- up_bias: bfloat16 [3072], P('fsdp'), may hold values from -6 to 6
- down_weight: bfloat16 [3072, 768], P('fsdp'), may hold values from -0.109375 to 0.109375
- down_bias: bfloat16 [768], P('fsdp'), may hold values from -4 to 4
- first_gain: bfloat16 [768], P('fsdp'), may hold values from 0.25 to 1.75
- first_shift: bfloat16 [768], P('fsdp'), may hold values from -4 to 4
- second_gain: bfloat16 [768], P('fsdp'), may hold values from 0.25 to 1.75
- second_shift: bfloat16 [768], P('fsdp'), may hold values from -4 to 4
- out_grad: bfloat16 [4, 2048, 768], P('fsdp', 'ctx'), may hold values from -6 to 6
Outputs:
- output: bfloat16 [4, 2048, 768], P('fsdp', 'ctx')
- input_gradient: float32 [4, 2048, 768], P('fsdp', 'ctx')
- in_weight_gradient: float32 [768, 2304], P('fsdp')
- in_bias_gradient: float32 [2304], P('fsdp')
- out_weight_gradient: float32 [768, 768], P('fsdp')
- out_bias_gradient: float32 [768], P('fsdp')
- up_weight_gradient: float32 [768, 3072], P('fsdp')
- up_bias_gradient: float32 [3072], P('fsdp')
- down_weight_gradient: float32 [3072, 768], P('fsdp')
- down_bias_gradient: float32 [768], P('fsdp')
- first_gain_gradient: float32 [768], P('fsdp')
- first_shift_gradient: float32 [768], P('fsdp')
- second_gain_gradient: float32 [768], P('fsdp')
- second_shift_gradient: float32 [768], P('fsdp')
Inputs may be any that keep to these rules, and one draw needn't show every extreme that they name: Each row holds every position of its sequence once, in runs of 128 consecutive rising positions that start at multiples of 128; the order of the runs differs from row to row.
All inputs are finite; a program needn't handle non-finite values.
Results may differ from a plain program's by a relative error of at most 0.018.
Values may be sent and summed in bfloat16 or wider, within the bound.
No kernel may reach another device: no remote copies, remote signals or barrier semaphores. Data moves between devices by JAX's collectives and lax.ppermute only.
A program may use at most 192 MiB of HBM per device.

v0:
```python
import math
import jax
import jax.numpy as jnp
from jax import lax
from jax.sharding import PartitionSpec as P

HEAD = 64
ROT = 16
NEG = -1e30
EPS = 1e-05


def from_behind(x, axis, by):
    size = lax.axis_size(axis)
    return lax.ppermute(x, axis, [(i, (i + by) % size) for i in range(size)])


def layer_norm(values, gain, shift):
    mean = jnp.mean(values, -1, keepdims=True)
    centred = values - mean
    spread = jnp.mean(centred * centred, -1, keepdims=True)
    return centred * lax.rsqrt(spread + EPS) * gain + shift


def turn_tables(positions):
    ladder = 10000.0 ** (-jnp.arange(0, ROT, 2, dtype=jnp.float32) / ROT)
    angle = positions.astype(jnp.float32)[..., None] * ladder
    angle = jnp.concatenate([angle, angle], -1)
    return (jnp.cos(angle), jnp.sin(angle))


def rotate(values, cosine, sine):
    half = ROT // 2
    part = values[..., :ROT]
    turned = jnp.concatenate([-part[..., half:], part[..., :half]], -1)
    part = part * cosine[..., None, :] + turned * sine[..., None, :]
    return jnp.concatenate([part, values[..., ROT:]], -1)


def across(left, right):
    return lax.dot_general(
        left, right, (((0,), (0,)), ((), ())), preferred_element_type=jnp.float32
    )


def against(left, right):
    return lax.dot_general(
        left, right, (((1,), (1,)), ((), ())), preferred_element_type=jnp.float32
    )


def softmax_step(carry, queries, query_pos, keys, values, key_pos, scale):
    peak, total, summed = carry
    scores = jnp.einsum("qhd,khd->hqk", queries, keys, preferred_element_type=jnp.float32) * scale
    allowed = (key_pos[None, :] <= query_pos[:, None])[None]
    new_peak = jnp.maximum(peak, jnp.max(jnp.where(allowed, scores, NEG), -1))
    weights = jnp.where(allowed, jnp.exp(scores - new_peak[..., None]), 0.0)
    fade = jnp.exp(peak - new_peak)
    total = total * fade + jnp.sum(weights, -1)
    added = jnp.einsum(
        "hqk,khd->qhd", weights.astype(jnp.bfloat16), values, preferred_element_type=jnp.float32
    )
    summed = summed * jnp.transpose(fade)[:, :, None] + added
    return (new_peak, total, summed)


def gradient_step(
    state, queries, query_pos, outs_back, log_total, spread, keys, values, key_pos, scale
):
    back_query, back_key, back_value = state
    scores = jnp.einsum("qhd,khd->hqk", queries, keys, preferred_element_type=jnp.float32) * scale
    allowed = (key_pos[None, :] <= query_pos[:, None])[None]
    probs = jnp.where(allowed, jnp.exp(scores - log_total[..., None]), 0.0)
    back_probs = jnp.einsum("qhd,khd->hqk", outs_back, values, preferred_element_type=jnp.float32)
    back_scores = (probs * (back_probs - spread[..., None])).astype(jnp.bfloat16)
    back_query = (
        back_query
        + jnp.einsum("hqk,khd->qhd", back_scores, keys, preferred_element_type=jnp.float32) * scale
    )
    back_key = (
        back_key
        + jnp.einsum("hqk,qhd->khd", back_scores, queries, preferred_element_type=jnp.float32)
        * scale
    )
    back_value = back_value + jnp.einsum(
        "hqk,qhd->khd", probs.astype(jnp.bfloat16), outs_back, preferred_element_type=jnp.float32
    )
    return (back_query, back_key, back_value)


def on_device(
    inputs,
    positions,
    in_weight,
    in_bias,
    out_weight,
    out_bias,
    up_weight,
    up_bias,
    down_weight,
    down_bias,
    first_gain,
    first_shift,
    second_gain,
    second_shift,
    out_grad,
):
    gathered = (
        lax.all_gather(in_weight, "fsdp", axis=0, tiled=True),
        lax.all_gather(in_bias, "fsdp", axis=0, tiled=True),
        lax.all_gather(out_weight, "fsdp", axis=0, tiled=True),
        lax.all_gather(out_bias, "fsdp", axis=0, tiled=True),
        lax.all_gather(up_weight, "fsdp", axis=0, tiled=True),
        lax.all_gather(up_bias, "fsdp", axis=0, tiled=True),
        lax.all_gather(down_weight, "fsdp", axis=0, tiled=True),
        lax.all_gather(down_bias, "fsdp", axis=0, tiled=True),
        lax.all_gather(first_gain, "fsdp", axis=0, tiled=True),
        lax.all_gather(first_shift, "fsdp", axis=0, tiled=True),
        lax.all_gather(second_gain, "fsdp", axis=0, tiled=True),
        lax.all_gather(second_shift, "fsdp", axis=0, tiled=True),
    )
    (
        full_in,
        full_in_bias,
        full_out,
        full_out_bias,
        full_up,
        full_up_bias,
        full_down,
        full_down_bias,
        gain_one,
        shift_one,
        gain_two,
        shift_two,
    ) = gathered
    tokens = inputs.shape[1]
    width = inputs.shape[2]
    heads = width // HEAD
    scale = 1.0 / math.sqrt(HEAD)
    query_pos = positions[0]
    all_pos = lax.all_gather(query_pos, "ctx", axis=0, tiled=True)
    resid = inputs[0].astype(jnp.float32)

    def norms(values, gain_a, shift_a, gain_b, shift_b):
        return (layer_norm(values, gain_a, shift_a), layer_norm(values, gain_b, shift_b))

    (normed_one, normed_two), norm_back = jax.vjp(
        norms,
        resid,
        gain_one.astype(jnp.float32),
        shift_one.astype(jnp.float32),
        gain_two.astype(jnp.float32),
        shift_two.astype(jnp.float32),
    )
    first = normed_one.astype(jnp.bfloat16)
    second = normed_two.astype(jnp.bfloat16)
    projected = jnp.dot(first, full_in, preferred_element_type=jnp.float32) + full_in_bias.astype(
        jnp.float32
    )
    projected = projected.reshape(tokens, 3, heads, HEAD)
    cosine, sine = turn_tables(query_pos)
    queries = rotate(projected[:, 0], cosine, sine).astype(jnp.bfloat16)
    keys = rotate(projected[:, 1], cosine, sine).astype(jnp.bfloat16)
    values = projected[:, 2].astype(jnp.bfloat16)
    start_state = (
        jnp.full((heads, tokens), NEG, jnp.float32),
        jnp.zeros((heads, tokens), jnp.float32),
        jnp.zeros((tokens, heads, HEAD), jnp.float32),
    )
    carry = start_state
    key_piece = lax.all_gather(keys, "ctx", axis=0, tiled=True)
    value_piece = lax.all_gather(values, "ctx", axis=0, tiled=True)
    count = key_piece.shape[0]
    size = 512

    def one_block(inner, offset):
        key_block = lax.dynamic_slice_in_dim(key_piece, offset, size, 0)
        value_block = lax.dynamic_slice_in_dim(value_piece, offset, size, 0)
        key_pos = lax.dynamic_slice_in_dim(all_pos, offset, size, 0)
        result = softmax_step(inner, queries, query_pos, key_block, value_block, key_pos, scale)
        return (result, None)

    carry, _ = lax.scan(one_block, carry, jnp.arange(0, count, size, dtype=jnp.int32))
    peak, total, summed = carry
    attended = summed / jnp.transpose(total)[:, :, None]
    log_total = peak + jnp.log(total)
    mixed = attended.reshape(tokens, width).astype(jnp.bfloat16)
    up = jnp.dot(second, full_up, preferred_element_type=jnp.float32) + full_up_bias.astype(
        jnp.float32
    )
    activated, gelu_back = jax.vjp(lambda value: jax.nn.gelu(value, approximate=False), up)
    activated = activated.astype(jnp.bfloat16)
    branch_attn = jnp.dot(
        mixed, full_out, preferred_element_type=jnp.float32
    ) + full_out_bias.astype(jnp.float32)
    branch_ff = jnp.dot(
        activated, full_down, preferred_element_type=jnp.float32
    ) + full_down_bias.astype(jnp.float32)
    output = resid + branch_attn + branch_ff
    cotangent = out_grad[0]
    back_out = cotangent.astype(jnp.float32)
    bias_sum = jnp.sum(back_out, 0)
    out_weight_part = across(mixed, cotangent)
    down_weight_part = across(activated, cotangent)
    back_mixed = against(cotangent, full_out).astype(jnp.bfloat16)
    back_active = against(cotangent, full_down)
    back_up = gelu_back(back_active)[0].astype(jnp.bfloat16)
    up_weight_part = across(second, back_up)
    up_bias_part = jnp.sum(back_up.astype(jnp.float32), 0)
    back_second = against(back_up, full_up)
    outs_back = back_mixed.reshape(tokens, heads, HEAD)
    spread = jnp.einsum("qhd,qhd->hq", outs_back.astype(jnp.float32), attended)
    cycle_size = lax.axis_size("ctx")
    here = lax.axis_index("ctx")
    zeros = jnp.zeros((tokens, heads, HEAD), jnp.float32)

    def key_turn(turn, state):
        moving_key, moving_value, back_key, back_value, back_query = state
        owner = (here - turn) % cycle_size
        key_pos = lax.dynamic_slice_in_dim(all_pos, owner * tokens, tokens, 0)
        back_query, back_key, back_value = gradient_step(
            (back_query, back_key, back_value),
            queries,
            query_pos,
            outs_back,
            log_total,
            spread,
            moving_key,
            moving_value,
            key_pos,
            scale,
        )
        moving_key, moving_value = from_behind((moving_key, moving_value), "ctx", 1)
        back_key, back_value = (
            from_behind(back_key.astype(jnp.bfloat16), "ctx", 1).astype(back_key.dtype),
            from_behind(back_value.astype(jnp.bfloat16), "ctx", 1).astype(back_value.dtype),
        )
        return (moving_key, moving_value, back_key, back_value, back_query)

    final = lax.fori_loop(0, cycle_size, key_turn, (keys, values, zeros, zeros, zeros))
    back_query, back_key, back_value = (final[4], final[2], final[3])
    back_query = rotate(back_query, cosine, -sine)
    back_key = rotate(back_key, cosine, -sine)
    back_projected = (
        jnp.stack([back_query, back_key, back_value], 1)
        .reshape(tokens, 3 * width)
        .astype(jnp.bfloat16)
    )
    in_weight_part = across(first, back_projected)
    in_bias_part = jnp.sum(back_projected.astype(jnp.float32), 0)
    back_first = against(back_projected, full_in)
    back_resid, gain_one_part, shift_one_part, gain_two_part, shift_two_part = norm_back(
        (back_first, back_second)
    )
    input_gradient = back_out + back_resid
    shares = (
        lax.psum_scatter(
            in_weight_part.astype(jnp.bfloat16), "fsdp", scatter_dimension=0, tiled=True
        ).astype(jnp.float32),
        lax.psum_scatter(
            in_bias_part.astype(jnp.bfloat16), "fsdp", scatter_dimension=0, tiled=True
        ).astype(jnp.float32),
        lax.psum_scatter(
            out_weight_part.astype(jnp.bfloat16), "fsdp", scatter_dimension=0, tiled=True
        ).astype(jnp.float32),
        lax.psum_scatter(
            bias_sum.astype(jnp.bfloat16), "fsdp", scatter_dimension=0, tiled=True
        ).astype(jnp.float32),
        lax.psum_scatter(
            up_weight_part.astype(jnp.bfloat16), "fsdp", scatter_dimension=0, tiled=True
        ).astype(jnp.float32),
        lax.psum_scatter(
            up_bias_part.astype(jnp.bfloat16), "fsdp", scatter_dimension=0, tiled=True
        ).astype(jnp.float32),
        lax.psum_scatter(
            down_weight_part.astype(jnp.bfloat16), "fsdp", scatter_dimension=0, tiled=True
        ).astype(jnp.float32),
        lax.psum_scatter(
            gain_one_part.astype(jnp.bfloat16), "fsdp", scatter_dimension=0, tiled=True
        ).astype(jnp.float32),
        lax.psum_scatter(
            shift_one_part.astype(jnp.bfloat16), "fsdp", scatter_dimension=0, tiled=True
        ).astype(jnp.float32),
        lax.psum_scatter(
            gain_two_part.astype(jnp.bfloat16), "fsdp", scatter_dimension=0, tiled=True
        ).astype(jnp.float32),
        lax.psum_scatter(
            shift_two_part.astype(jnp.bfloat16), "fsdp", scatter_dimension=0, tiled=True
        ).astype(jnp.float32),
    )
    totals = (
        lax.psum(shares[0].astype(jnp.bfloat16), "ctx").astype(jnp.float32),
        lax.psum(shares[1].astype(jnp.bfloat16), "ctx").astype(jnp.float32),
        lax.psum(shares[2].astype(jnp.bfloat16), "ctx").astype(jnp.float32),
        lax.psum(shares[3].astype(jnp.bfloat16), "ctx").astype(jnp.float32),
        lax.psum(shares[4].astype(jnp.bfloat16), "ctx").astype(jnp.float32),
        lax.psum(shares[5].astype(jnp.bfloat16), "ctx").astype(jnp.float32),
        lax.psum(shares[6].astype(jnp.bfloat16), "ctx").astype(jnp.float32),
        lax.psum(shares[7].astype(jnp.bfloat16), "ctx").astype(jnp.float32),
        lax.psum(shares[8].astype(jnp.bfloat16), "ctx").astype(jnp.float32),
        lax.psum(shares[9].astype(jnp.bfloat16), "ctx").astype(jnp.float32),
        lax.psum(shares[10].astype(jnp.bfloat16), "ctx").astype(jnp.float32),
    )
    return (
        output.astype(jnp.bfloat16)[None],
        input_gradient[None],
        totals[0],
        totals[1],
        totals[2],
        totals[3],
        totals[4],
        totals[5],
        totals[6],
        totals[3],
        totals[7],
        totals[8],
        totals[9],
        totals[10],
    )


def solution(mesh):
    return jax.shard_map(
        on_device,
        mesh=mesh,
        in_specs=(
            P("fsdp", "ctx", None),
            P("fsdp", "ctx"),
            P("fsdp", None),
            P("fsdp"),
            P("fsdp", None),
            P("fsdp"),
            P("fsdp", None),
            P("fsdp"),
            P("fsdp", None),
            P("fsdp"),
            P("fsdp"),
            P("fsdp"),
            P("fsdp"),
            P("fsdp"),
            P("fsdp", "ctx", None),
        ),
        out_specs=(
            P("fsdp", "ctx", None),
            P("fsdp", "ctx", None),
            P("fsdp", None),
            P("fsdp"),
            P("fsdp", None),
            P("fsdp"),
            P("fsdp", None),
            P("fsdp"),
            P("fsdp", None),
            P("fsdp"),
            P("fsdp"),
            P("fsdp"),
            P("fsdp"),
            P("fsdp"),
        ),
        check_vma=False,
    )
```

profile of v0, /device:TPU:0, one launch (start us, length us, event | category | flops | bytes accessed | tf_op | source)
XLA Modules:
  0.0 707.0 jit_solution(10681487738134994407)
XLA Ops:
  14.8 18.4 %all-reduce.17 = (bf16[768]{0:T(1024)(128)(2,1)}, bf16[768]{0:T(1024)(128)(2,1)}, bf16[2304]{0:T(1024)(128)(2,1)S(1)}, bf16[768]{0:T(1024)(128)(2,1)S(1)}, bf16[768]{0:T(1024)(128)(2,1)S(1)}) all-reduce(bf16[768]{0:T(1024)(128)(2,1)S(1)} %dynamic-update-slice.5, ...), channel_id=1, replica_groups=mesh['fsdp'=4,'ctx'=8] {'fsdp'}, use_global_device_ids=true, to_apply=%add.5 | all-reduce | flops 5376 | bytes 21504
  37.1 22.8 %all-gather.10.cloned.1.call-done = bf16[768,2304]{1,0:T(8,128)(2,1)} async-done(((bf16[192,2304]{1,0:T(8,128)(2,1)}), bf16[768,2304]{1,0:T(8,128)(2,1)}) %all-gather.10.cloned.1.call-update) | async-done | bytes 3538960 | tf_op jit(solution)/shard_map/all_gather | solution.py:109
  59.9 4.7 convolution_add_fusion
  71.0 12.8 %all-gather = s32[1,2048]{1,0:T(1,128)} all-gather(s32[1,256]{1,0:T(1,128)} %param.20), channel_id=2, replica_groups=mesh['fsdp'=4,'ctx'=8] {'ctx'}, dimensions={1}, use_global_device_ids=true | all-gather | bytes 9216 | tf_op jit(solution)/shard_map/all_gather | solution.py:141
  85.9 8.1 %all-gather.2 = bf16[4,1,768]{2,1,0:T(2,128)(2,1)S(1)} all-gather(bf16[1,1,768]{2,1,0:T(2,128)(2,1)S(1)} %reshape.293), channel_id=1, replica_groups=mesh['fsdp'=4,'ctx'=8] {'fsdp'}, dimensions={0}, use_global_device_ids=true | all-gather | bytes 7680 | tf_op jit(solution)/shard_map/all_gather | solution.py:114
  94.1 13.7 %all-gather.12.cloned.1.call-done = bf16[2048,12,64]{0,2,1:T(8,128)(2,1)} async-done(((bf16[256,12,64]{0,2,1:T(8,128)(2,1)}), bf16[2048,12,64]{0,2,1:T(8,128)(2,1)}) %all-gather.12.cloned.1.call-update) | async-done | bytes 3145744 | tf_op jit(solution)/shard_map/all_gather | solution.py:171
  107.7 41.4 %all-gather.20.cloned.1.call-done = bf16[2048,1,12,64]{0,3,2,1:T(8,128)(2,1)} async-done(((bf16[256,1,12,64]{0,3,2,1:T(8,128)(2,1)}), bf16[2048,1,12,64]{0,3,2,1:T(8,128)(2,1)}) %all-gather.20.cloned.1.call-update) | async-done | bytes 3145744 | tf_op jit(solution)/shard_map/all_gather | solution.py:172
  149.1 64.1 %while.39 = (s32[]{:T(128)}, f32[12,256]{1,0:T(8,128)S(1)}, f32[12,256]{1,0:T(8,128)S(1)}, f32[256,12,64]{0,2,1:T(8,128)S(1)}, s32[4]{0:T(128)S(1)}, /*index=5*/...) while((s32[]{:T(128)}, f32[12,256]{1,0:T(8,128)S(1)}, ...), condition=%wide.region_5.6_spmd.clone, body=%wide.region_2.5_spmd.clone.sunk | while | flops 420694016 | bytes 48307420 | solution.py:183
  153.2 5.7 fusion.173
  158.9 4.8 fusion.177
  169.2 5.5 fusion.173
  174.7 4.8 fusion.177
  185.8 5.5 fusion.173
  191.3 4.8 fusion.177
  201.6 5.4 fusion.173
  207.1 4.7 fusion.177
  215.2 11.6 %multiply_convert_fusion.1 = (bf16[256,3072]{1,0:T(8,128)(2,1)S(1)}, f32[256,3072]{1,0:T(8,128)}, f32[256,3072]{1,0:T(8,128)}) fusion(f32[3072]{0:T(1024)S(1)} %bitcast.232, bf16[768,3072]{1,0:T(8,128)(2,1)} %all-gather.16.cloned.1.call-done, bf16[1,256,768]{2,1,0:T(8,128)(2,1)S(1)} %copy-done.3, f32[768]{0:T(1024)S(1)} %convert_element_type.251, ...), kind=kOutput, calls=%fused_computation.54 | convolution fusion | flops 1261043712 | bytes 12996608 | tf_op jit(solution)/shard_map/dot_general | solution.py:188
  226.7 38.2 %all-gather.18.cloned.1.call-done = bf16[3072,768]{1,0:T(8,128)(2,1)} async-done(((bf16[768,768]{1,0:T(8,128)(2,1)}), bf16[3072,768]{1,0:T(8,128)(2,1)}) %all-gather.18.cloned.1.call-update) | async-done | bytes 4718608 | tf_op jit(solution)/shard_map/all_gather | solution.py:115
  264.9 6.8 fusion.119
  272.9 3.7 convolution_convert_fusion.1
  276.7 17.6 %all-gather.14.cloned.1.call-done = bf16[768,768]{1,0:T(8,128)(2,1)} async-done(((bf16[192,768]{1,0:T(8,128)(2,1)}), bf16[768,768]{1,0:T(8,128)(2,1)}) %all-gather.14.cloned.1.call-update) | async-done | bytes 1179664 | tf_op jit(solution)/shard_map/all_gather | solution.py:111
  300.7 3.5 convolution_convert_fusion
  307.7 244.7 %while.40 = (s32[]{:T(128)}, bf16[256,12,64]{0,2,1:T(8,128)(2,1)}, bf16[256,12,64]{0,2,1:T(8,128)(2,1)}, f32[256,12,64]{0,2,1:T(8,128)S(1)}, f32[256,12,64]{0,2,...) while((s32[]{:T(128)}, bf16[256,12,64]{0,2,1:T(8,128)(2,1)}, ...), condition=%wide.region_9.10_spmd.clone, body=%wide.region_8.9_spmd.clone.sunk | while | flops 513605632 | bytes 40837772 | solution.py:240
  334.1 4.2 collective-permute-done.1
  352.6 3.6 collective-permute-done.2
  357.3 3.1 collective-permute-done.3
  364.7 4.2 collective-permute-done.1
  381.9 5.1 collective-permute-done.2
  388.0 3.1 collective-permute-done.3
  395.4 4.2 collective-permute-done.1
  412.6 5.0 collective-permute-done.2
  426.0 4.2 collective-permute-done.1
  443.1 5.1 collective-permute-done.2
  456.6 4.2 collective-permute-done.1
  473.6 5.1 collective-permute-done.2
  479.8 3.1 collective-permute-done.3
  487.1 4.2 collective-permute-done.1
  504.2 5.1 collective-permute-done.2
  517.7 4.2 collective-permute-done.1
  534.7 5.1 collective-permute-done.2
  548.2 4.2 collective-permute-done.1
  556.2 3.2 convolution_convert_fusion.2
  563.0 4.8 fusion.121
  570.0 34.4 %reduce-scatter.5.cloned.1.call-done = bf16[192,2304]{1,0:T(8,128)(2,1)} async-done(((bf16[768,2304]{1,0:T(8,128)(2,1)}), bf16[192,2304]{1,0:T(8,128)(2,1)}) %reduce-scatter.5.cloned.1.call-update) | async-done | bytes 884752 | tf_op jit(solution)/shard_map/reduce_scatter | solution.py:257
  606.4 15.3 %all-reduce.16 = (bf16[768]{0:T(1024)(128)(2,1)S(1)}, bf16[768]{0:T(1024)(128)(2,1)S(1)}, bf16[2304]{0:T(1024)(128)(2,1)S(1)}, bf16[768]{0:T(1024)(128)(2,1)S(1)...) all-reduce(bf16[768]{0:T(1024)(128)(2,1)S(1)} %dynamic-update-slice, ...), channel_id=1, replica_groups=mesh['fsdp'=4,'ctx'=8] {'fsdp'}, use_global_device_ids=true, to_apply=%add.6 | all-reduce | flops 10752 | bytes 43008
  622.3 15.3 %all-reduce.14 = (bf16[576]{0:T(1024)(128)(2,1)S(1)}, bf16[192]{0:T(256)(128)(2,1)S(1)}, bf16[768]{0:T(1024)(128)(2,1)S(1)}, bf16[192]{0:T(256)(128)(2,1)S(1)}, ...) all-reduce(bf16[576]{0:T(1024)(128)(2,1)S(1)} %dynamic-slice.8, ...), channel_id=1, replica_groups=mesh['fsdp'=4,'ctx'=8] {'ctx'}, use_global_device_ids=true, to_apply=%region_16.17 | all-reduce | flops 2304 | bytes 9216 | tf_op jit(solution)/shard_map/psum | solution.py:293
  641.1 3.9 convolution_add_fusion.3
  647.7 45.3 %all-reduce.20.cloned.1.call-done = (bf16[192,2304]{1,0:T(8,128)(2,1)}, bf16[192,768]{1,0:T(8,128)(2,1)}, bf16[192,3072]{1,0:T(8,128)(2,1)}, bf16[768,768]{1,0:T(8,128)(2,1)}) async-done(((bf16[192,2304]{1,0:T(8,128)(2,1)}, bf16[192,768]{1,0:T(8,128)(2,1)}, bf16[192,3072]{1,0:T(8,128)(2,1)}, bf16[768,768]{1,0:T(8,128)(2,1)}), (bf16[192,2304]{1,0:T(8,128)(2,1)}, bf16[192,768]{1,0:T(8,128)(2,1)}, ...) | async-done | bytes 3538960 | tf_op jit(solution)/shard_map/psum | solution.py:292
  (450 shorter events, 236.7 us)
Async XLA Ops:
  7.2 52.8 %all-gather.10.cloned.1.call-start = ((), (), s32[]{:S(2)}) async-start(), calls=%async_computation.4 | async-start | bytes 4423680 | tf_op jit(solution)/shard_map/all_gather | solution.py:109
  7.9 99.8 %all-gather.12.cloned.1.call-start = ((), (), s32[]{:S(2)}) async-start(), calls=%async_computation.5 | async-start | bytes 3538944 | tf_op jit(solution)/shard_map/all_gather | solution.py:171
  68.4 80.7 %all-gather.20.cloned.1.call-start = ((), (), s32[]{:S(2)}) async-start(), calls=%async_computation.13 | async-start | bytes 3538944 | tf_op jit(solution)/shard_map/all_gather | solution.py:172
  69.2 145.9 %all-gather.16.cloned.1.call-start = ((), (), s32[]{:S(2)}) async-start(), calls=%async_computation.7 | async-start | bytes 5898240 | tf_op jit(solution)/shard_map/all_gather | solution.py:113
  69.8 195.1 %all-gather.18.cloned.1.call-start = ((), (), s32[]{:S(2)}) async-start(), calls=%async_computation.8 | async-start | bytes 5898240 | tf_op jit(solution)/shard_map/all_gather | solution.py:115
  70.4 223.9 %all-gather.14.cloned.1.call-start = ((), (), s32[]{:S(2)}) async-start(), calls=%async_computation.6 | async-start | bytes 1474560 | tf_op jit(solution)/shard_map/all_gather | solution.py:111
  71.0 499.0 %reduce-scatter.7.cloned.1.call-start = ((), (), s32[]{:S(2)}) async-start(), calls=%async_computation.10 | async-start | bytes 1474560 | tf_op jit(solution)/shard_map/reduce_scatter | solution.py:263
  84.5 187.2 %copy-start.25 = (f32[768]{0:T(1024)}, f32[768]{0:T(1024)S(1)}, u32[]{:S(2)}) copy-start(f32[768]{0:T(1024)S(1)} %convert_element_type.250) | copy-start | bytes 9220
  149.1 64.3 %copy-start.4 = (bf16[1,256,768]{2,1,0:T(8,128)(2,1)S(1)}, bf16[1,256,768]{2,1,0:T(8,128)(2,1)}, u32[]{:S(2)}) copy-start(bf16[1,256,768]{2,1,0:T(8,128)(2,1)} %param.33) | copy-start | bytes 1179652
  214.9 355.1 %reduce-scatter.9.cloned.1.call-start = ((), (), s32[]{:S(2)}) async-start(), calls=%async_computation.11 | async-start | bytes 5898240 | tf_op jit(solution)/shard_map/reduce_scatter | solution.py:269
  226.7 74.0 %copy-start.10 = (bf16[256,3072]{1,0:T(8,128)(2,1)}, bf16[256,3072]{1,0:T(8,128)(2,1)S(1)}, u32[]{:S(2)}) copy-start(bf16[256,3072]{1,0:T(8,128)(2,1)S(1)} %get-tuple-element.560) | copy-start | bytes 4718596
  276.6 293.4 %reduce-scatter.11.cloned.1.call-start = ((), (), s32[]{:S(2)}) async-start(), calls=%async_computation.12 | async-start | bytes 5898240 | tf_op jit(solution)/shard_map/reduce_scatter | solution.py:275
  304.3 300.2 %reduce-scatter.5.cloned.1.call-start = ((), (), s32[]{:S(2)}) async-start(), calls=%async_computation.9 | async-start | bytes 4423680 | tf_op jit(solution)/shard_map/reduce_scatter | solution.py:257
  307.7 247.0 %copy-start.28 = (f32[256,16]{0,1:T(8,128)S(1)}, f32[256,16]{0,1:T(8,128)}, u32[]{:S(2)}) copy-start(f32[256,16]{0,1:T(8,128)} %copy-done.27) | copy-start | bytes 49156
  316.4 9.3 %collective-permute-start.2 = (bf16[256,12,64]{0,2,1:T(8,128)(2,1)}, bf16[256,12,64]{0,2,1:T(8,128)(2,1)}, u32[]{:S(2)}, u32[]{:S(2)}) collective-permute-start(bf16[256,12,64]{0,2,1:T(8,128)(2,1)} %fusion.189), channel_id=1, source_target_pairs={{0,1},{1,2},{2,3},{3,4},{4,5},{5,6},{6,7},{7,0},{8,9},{9,10},{10,1... | collective-permute-start | bytes 1179656 | tf_op jit(solution)/shard_map/while/body/eval_jaxpr/ppermute | solution.py:15
  319.0 10.9 %collective-permute-start.3 = (bf16[256,12,64]{0,2,1:T(8,128)(2,1)}, bf16[256,12,64]{0,2,1:T(8,128)(2,1)}, u32[]{:S(2)}, u32[]{:S(2)}) collective-permute-start(bf16[256,12,64]{0,2,1:T(8,128)(2,1)} %fusion.190), channel_id=1, source_target_pairs={{0,1},{1,2},{2,3},{3,4},{4,5},{5,6},{6,7},{7,0},{8,9},{9,10},{10,1... | collective-permute-start | bytes 1179656 | tf_op jit(solution)/shard_map/while/body/eval_jaxpr/ppermute | solution.py:15
  320.5 13.6 %collective-permute-start = (bf16[256,12,64]{0,2,1:T(8,128)(2,1)S(1)}, bf16[256,12,64]{0,2,1:T(8,128)(2,1)}, u32[]{:S(2)}, u32[]{:S(2)}) collective-permute-start(bf16[256,12,64]{0,2,1:T(8,128)(2,1)S(1)} %copy.76), channel_id=1, source_target_pairs={{0,1},{1,2},{2,3},{3,4},{4,5},{5,6},{6,7},{7,0},{8,9},{9,10},{10,1... | collective-permute-start | bytes 1179656 | tf_op jit(solution)/shard_map/while/body/eval_jaxpr/ppermute | solution.py:15
  320.6 17.7 %collective-permute-start.1 = (bf16[256,12,64]{0,2,1:T(8,128)(2,1)}, bf16[256,12,64]{0,2,1:T(8,128)(2,1)}, u32[]{:S(2)}, u32[]{:S(2)}) collective-permute-start(bf16[256,12,64]{0,2,1:T(8,128)(2,1)} %copy.77), channel_id=1, source_target_pairs={{0,1},{1,2},{2,3},{3,4},{4,5},{5,6},{6,7},{7,0},{8,9},{9,10},{10,1... | collective-permute-start | bytes 1179656 | tf_op jit(solution)/shard_map/while/body/eval_jaxpr/ppermute | solution.py:15
  346.9 9.3 %collective-permute-start.2 = (bf16[256,12,64]{0,2,1:T(8,128)(2,1)}, bf16[256,12,64]{0,2,1:T(8,128)(2,1)}, u32[]{:S(2)}, u32[]{:S(2)}) collective-permute-start(bf16[256,12,64]{0,2,1:T(8,128)(2,1)} %fusion.189), channel_id=1, source_target_pairs={{0,1},{1,2},{2,3},{3,4},{4,5},{5,6},{6,7},{7,0},{8,9},{9,10},{10,1... | collective-permute-start | bytes 1179656 | tf_op jit(solution)/shard_map/while/body/eval_jaxpr/ppermute | solution.py:15
  349.6 10.9 %collective-permute-start.3 = (bf16[256,12,64]{0,2,1:T(8,128)(2,1)}, bf16[256,12,64]{0,2,1:T(8,128)(2,1)}, u32[]{:S(2)}, u32[]{:S(2)}) collective-permute-start(bf16[256,12,64]{0,2,1:T(8,128)(2,1)} %fusion.190), channel_id=1, source_target_pairs={{0,1},{1,2},{2,3},{3,4},{4,5},{5,6},{6,7},{7,0},{8,9},{9,10},{10,1... | collective-permute-start | bytes 1179656 | tf_op jit(solution)/shard_map/while/body/eval_jaxpr/ppermute | solution.py:15
  349.6 15.1 %collective-permute-start = (bf16[256,12,64]{0,2,1:T(8,128)(2,1)S(1)}, bf16[256,12,64]{0,2,1:T(8,128)(2,1)}, u32[]{:S(2)}, u32[]{:S(2)}) collective-permute-start(bf16[256,12,64]{0,2,1:T(8,128)(2,1)S(1)} %copy.76), channel_id=1, source_target_pairs={{0,1},{1,2},{2,3},{3,4},{4,5},{5,6},{6,7},{7,0},{8,9},{9,10},{10,1... | collective-permute-start | bytes 1179656 | tf_op jit(solution)/shard_map/while/body/eval_jaxpr/ppermute | solution.py:15
  349.6 19.3 %collective-permute-start.1 = (bf16[256,12,64]{0,2,1:T(8,128)(2,1)}, bf16[256,12,64]{0,2,1:T(8,128)(2,1)}, u32[]{:S(2)}, u32[]{:S(2)}) collective-permute-start(bf16[256,12,64]{0,2,1:T(8,128)(2,1)} %copy.77), channel_id=1, source_target_pairs={{0,1},{1,2},{2,3},{3,4},{4,5},{5,6},{6,7},{7,0},{8,9},{9,10},{10,1... | collective-permute-start | bytes 1179656 | tf_op jit(solution)/shard_map/while/body/eval_jaxpr/ppermute | solution.py:15
  377.6 9.3 %collective-permute-start.2 = (bf16[256,12,64]{0,2,1:T(8,128)(2,1)}, bf16[256,12,64]{0,2,1:T(8,128)(2,1)}, u32[]{:S(2)}, u32[]{:S(2)}) collective-permute-start(bf16[256,12,64]{0,2,1:T(8,128)(2,1)} %fusion.189), channel_id=1, source_target_pairs={{0,1},{1,2},{2,3},{3,4},{4,5},{5,6},{6,7},{7,0},{8,9},{9,10},{10,1... | collective-permute-start | bytes 1179656 | tf_op jit(solution)/shard_map/while/body/eval_jaxpr/ppermute | solution.py:15
  380.3 10.9 %collective-permute-start.3 = (bf16[256,12,64]{0,2,1:T(8,128)(2,1)}, bf16[256,12,64]{0,2,1:T(8,128)(2,1)}, u32[]{:S(2)}, u32[]{:S(2)}) collective-permute-start(bf16[256,12,64]{0,2,1:T(8,128)(2,1)} %fusion.190), channel_id=1, source_target_pairs={{0,1},{1,2},{2,3},{3,4},{4,5},{5,6},{6,7},{7,0},{8,9},{9,10},{10,1... | collective-permute-start | bytes 1179656 | tf_op jit(solution)/shard_map/while/body/eval_jaxpr/ppermute | solution.py:15
  380.3 15.1 %collective-permute-start = (bf16[256,12,64]{0,2,1:T(8,128)(2,1)S(1)}, bf16[256,12,64]{0,2,1:T(8,128)(2,1)}, u32[]{:S(2)}, u32[]{:S(2)}) collective-permute-start(bf16[256,12,64]{0,2,1:T(8,128)(2,1)S(1)} %copy.76), channel_id=1, source_target_pairs={{0,1},{1,2},{2,3},{3,4},{4,5},{5,6},{6,7},{7,0},{8,9},{9,10},{10,1... | collective-permute-start | bytes 1179656 | tf_op jit(solution)/shard_map/while/body/eval_jaxpr/ppermute | solution.py:15
  380.3 19.3 %collective-permute-start.1 = (bf16[256,12,64]{0,2,1:T(8,128)(2,1)}, bf16[256,12,64]{0,2,1:T(8,128)(2,1)}, u32[]{:S(2)}, u32[]{:S(2)}) collective-permute-start(bf16[256,12,64]{0,2,1:T(8,128)(2,1)} %copy.77), channel_id=1, source_target_pairs={{0,1},{1,2},{2,3},{3,4},{4,5},{5,6},{6,7},{7,0},{8,9},{9,10},{10,1... | collective-permute-start | bytes 1179656 | tf_op jit(solution)/shard_map/while/body/eval_jaxpr/ppermute | solution.py:15
  408.2 9.3 %collective-permute-start.2 = (bf16[256,12,64]{0,2,1:T(8,128)(2,1)}, bf16[256,12,64]{0,2,1:T(8,128)(2,1)}, u32[]{:S(2)}, u32[]{:S(2)}) collective-permute-start(bf16[256,12,64]{0,2,1:T(8,128)(2,1)} %fusion.189), channel_id=1, source_target_pairs={{0,1},{1,2},{2,3},{3,4},{4,5},{5,6},{6,7},{7,0},{8,9},{9,10},{10,1... | collective-permute-start | bytes 1179656 | tf_op jit(solution)/shard_map/while/body/eval_jaxpr/ppermute | solution.py:15
  410.9 10.8 %collective-permute-start.3 = (bf16[256,12,64]{0,2,1:T(8,128)(2,1)}, bf16[256,12,64]{0,2,1:T(8,128)(2,1)}, u32[]{:S(2)}, u32[]{:S(2)}) collective-permute-start(bf16[256,12,64]{0,2,1:T(8,128)(2,1)} %fusion.190), channel_id=1, source_target_pairs={{0,1},{1,2},{2,3},{3,4},{4,5},{5,6},{6,7},{7,0},{8,9},{9,10},{10,1... | collective-permute-start | bytes 1179656 | tf_op jit(solution)/shard_map/while/body/eval_jaxpr/ppermute | solution.py:15
  410.9 15.0 %collective-permute-start = (bf16[256,12,64]{0,2,1:T(8,128)(2,1)S(1)}, bf16[256,12,64]{0,2,1:T(8,128)(2,1)}, u32[]{:S(2)}, u32[]{:S(2)}) collective-permute-start(bf16[256,12,64]{0,2,1:T(8,128)(2,1)S(1)} %copy.76), channel_id=1, source_target_pairs={{0,1},{1,2},{2,3},{3,4},{4,5},{5,6},{6,7},{7,0},{8,9},{9,10},{10,1... | collective-permute-start | bytes 1179656 | tf_op jit(solution)/shard_map/while/body/eval_jaxpr/ppermute | solution.py:15
  410.9 19.2 %collective-permute-start.1 = (bf16[256,12,64]{0,2,1:T(8,128)(2,1)}, bf16[256,12,64]{0,2,1:T(8,128)(2,1)}, u32[]{:S(2)}, u32[]{:S(2)}) collective-permute-start(bf16[256,12,64]{0,2,1:T(8,128)(2,1)} %copy.77), channel_id=1, source_target_pairs={{0,1},{1,2},{2,3},{3,4},{4,5},{5,6},{6,7},{7,0},{8,9},{9,10},{10,1... | collective-permute-start | bytes 1179656 | tf_op jit(solution)/shard_map/while/body/eval_jaxpr/ppermute | solution.py:15
  438.8 9.3 %collective-permute-start.2 = (bf16[256,12,64]{0,2,1:T(8,128)(2,1)}, bf16[256,12,64]{0,2,1:T(8,128)(2,1)}, u32[]{:S(2)}, u32[]{:S(2)}) collective-permute-start(bf16[256,12,64]{0,2,1:T(8,128)(2,1)} %fusion.189), channel_id=1, source_target_pairs={{0,1},{1,2},{2,3},{3,4},{4,5},{5,6},{6,7},{7,0},{8,9},{9,10},{10,1... | collective-permute-start | bytes 1179656 | tf_op jit(solution)/shard_map/while/body/eval_jaxpr/ppermute | solution.py:15
  441.5 10.9 %collective-permute-start.3 = (bf16[256,12,64]{0,2,1:T(8,128)(2,1)}, bf16[256,12,64]{0,2,1:T(8,128)(2,1)}, u32[]{:S(2)}, u32[]{:S(2)}) collective-permute-start(bf16[256,12,64]{0,2,1:T(8,128)(2,1)} %fusion.190), channel_id=1, source_target_pairs={{0,1},{1,2},{2,3},{3,4},{4,5},{5,6},{6,7},{7,0},{8,9},{9,10},{10,1... | collective-permute-start | bytes 1179656 | tf_op jit(solution)/shard_map/while/body/eval_jaxpr/ppermute | solution.py:15
  441.5 15.1 %collective-permute-start = (bf16[256,12,64]{0,2,1:T(8,128)(2,1)S(1)}, bf16[256,12,64]{0,2,1:T(8,128)(2,1)}, u32[]{:S(2)}, u32[]{:S(2)}) collective-permute-start(bf16[256,12,64]{0,2,1:T(8,128)(2,1)S(1)} %copy.76), channel_id=1, source_target_pairs={{0,1},{1,2},{2,3},{3,4},{4,5},{5,6},{6,7},{7,0},{8,9},{9,10},{10,1... | collective-permute-start | bytes 1179656 | tf_op jit(solution)/shard_map/while/body/eval_jaxpr/ppermute | solution.py:15
  441.5 19.3 %collective-permute-start.1 = (bf16[256,12,64]{0,2,1:T(8,128)(2,1)}, bf16[256,12,64]{0,2,1:T(8,128)(2,1)}, u32[]{:S(2)}, u32[]{:S(2)}) collective-permute-start(bf16[256,12,64]{0,2,1:T(8,128)(2,1)} %copy.77), channel_id=1, source_target_pairs={{0,1},{1,2},{2,3},{3,4},{4,5},{5,6},{6,7},{7,0},{8,9},{9,10},{10,1... | collective-permute-start | bytes 1179656 | tf_op jit(solution)/shard_map/while/body/eval_jaxpr/ppermute | solution.py:15
  469.4 9.3 %collective-permute-start.2 = (bf16[256,12,64]{0,2,1:T(8,128)(2,1)}, bf16[256,12,64]{0,2,1:T(8,128)(2,1)}, u32[]{:S(2)}, u32[]{:S(2)}) collective-permute-start(bf16[256,12,64]{0,2,1:T(8,128)(2,1)} %fusion.189), channel_id=1, source_target_pairs={{0,1},{1,2},{2,3},{3,4},{4,5},{5,6},{6,7},{7,0},{8,9},{9,10},{10,1... | collective-permute-start | bytes 1179656 | tf_op jit(solution)/shard_map/while/body/eval_jaxpr/ppermute | solution.py:15
  472.0 10.9 %collective-permute-start.3 = (bf16[256,12,64]{0,2,1:T(8,128)(2,1)}, bf16[256,12,64]{0,2,1:T(8,128)(2,1)}, u32[]{:S(2)}, u32[]{:S(2)}) collective-permute-start(bf16[256,12,64]{0,2,1:T(8,128)(2,1)} %fusion.190), channel_id=1, source_target_pairs={{0,1},{1,2},{2,3},{3,4},{4,5},{5,6},{6,7},{7,0},{8,9},{9,10},{10,1... | collective-permute-start | bytes 1179656 | tf_op jit(solution)/shard_map/while/body/eval_jaxpr/ppermute | solution.py:15
  472.0 15.1 %collective-permute-start = (bf16[256,12,64]{0,2,1:T(8,128)(2,1)S(1)}, bf16[256,12,64]{0,2,1:T(8,128)(2,1)}, u32[]{:S(2)}, u32[]{:S(2)}) collective-permute-start(bf16[256,12,64]{0,2,1:T(8,128)(2,1)S(1)} %copy.76), channel_id=1, source_target_pairs={{0,1},{1,2},{2,3},{3,4},{4,5},{5,6},{6,7},{7,0},{8,9},{9,10},{10,1... | collective-permute-start | bytes 1179656 | tf_op jit(solution)/shard_map/while/body/eval_jaxpr/ppermute | solution.py:15
  472.0 19.3 %collective-permute-start.1 = (bf16[256,12,64]{0,2,1:T(8,128)(2,1)}, bf16[256,12,64]{0,2,1:T(8,128)(2,1)}, u32[]{:S(2)}, u32[]{:S(2)}) collective-permute-start(bf16[256,12,64]{0,2,1:T(8,128)(2,1)} %copy.77), channel_id=1, source_target_pairs={{0,1},{1,2},{2,3},{3,4},{4,5},{5,6},{6,7},{7,0},{8,9},{9,10},{10,1... | collective-permute-start | bytes 1179656 | tf_op jit(solution)/shard_map/while/body/eval_jaxpr/ppermute | solution.py:15
  499.9 9.3 %collective-permute-start.2 = (bf16[256,12,64]{0,2,1:T(8,128)(2,1)}, bf16[256,12,64]{0,2,1:T(8,128)(2,1)}, u32[]{:S(2)}, u32[]{:S(2)}) collective-permute-start(bf16[256,12,64]{0,2,1:T(8,128)(2,1)} %fusion.189), channel_id=1, source_target_pairs={{0,1},{1,2},{2,3},{3,4},{4,5},{5,6},{6,7},{7,0},{8,9},{9,10},{10,1... | collective-permute-start | bytes 1179656 | tf_op jit(solution)/shard_map/while/body/eval_jaxpr/ppermute | solution.py:15
  502.6 10.9 %collective-permute-start.3 = (bf16[256,12,64]{0,2,1:T(8,128)(2,1)}, bf16[256,12,64]{0,2,1:T(8,128)(2,1)}, u32[]{:S(2)}, u32[]{:S(2)}) collective-permute-start(bf16[256,12,64]{0,2,1:T(8,128)(2,1)} %fusion.190), channel_id=1, source_target_pairs={{0,1},{1,2},{2,3},{3,4},{4,5},{5,6},{6,7},{7,0},{8,9},{9,10},{10,1... | collective-permute-start | bytes 1179656 | tf_op jit(solution)/shard_map/while/body/eval_jaxpr/ppermute | solution.py:15
  502.6 15.1 %collective-permute-start = (bf16[256,12,64]{0,2,1:T(8,128)(2,1)S(1)}, bf16[256,12,64]{0,2,1:T(8,128)(2,1)}, u32[]{:S(2)}, u32[]{:S(2)}) collective-permute-start(bf16[256,12,64]{0,2,1:T(8,128)(2,1)S(1)} %copy.76), channel_id=1, source_target_pairs={{0,1},{1,2},{2,3},{3,4},{4,5},{5,6},{6,7},{7,0},{8,9},{9,10},{10,1... | collective-permute-start | bytes 1179656 | tf_op jit(solution)/shard_map/while/body/eval_jaxpr/ppermute | solution.py:15
  502.6 19.3 %collective-permute-start.1 = (bf16[256,12,64]{0,2,1:T(8,128)(2,1)}, bf16[256,12,64]{0,2,1:T(8,128)(2,1)}, u32[]{:S(2)}, u32[]{:S(2)}) collective-permute-start(bf16[256,12,64]{0,2,1:T(8,128)(2,1)} %copy.77), channel_id=1, source_target_pairs={{0,1},{1,2},{2,3},{3,4},{4,5},{5,6},{6,7},{7,0},{8,9},{9,10},{10,1... | collective-permute-start | bytes 1179656 | tf_op jit(solution)/shard_map/while/body/eval_jaxpr/ppermute | solution.py:15
  530.5 9.3 %collective-permute-start.2 = (bf16[256,12,64]{0,2,1:T(8,128)(2,1)}, bf16[256,12,64]{0,2,1:T(8,128)(2,1)}, u32[]{:S(2)}, u32[]{:S(2)}) collective-permute-start(bf16[256,12,64]{0,2,1:T(8,128)(2,1)} %fusion.189), channel_id=1, source_target_pairs={{0,1},{1,2},{2,3},{3,4},{4,5},{5,6},{6,7},{7,0},{8,9},{9,10},{10,1... | collective-permute-start | bytes 1179656 | tf_op jit(solution)/shard_map/while/body/eval_jaxpr/ppermute | solution.py:15
  533.1 10.9 %collective-permute-start.3 = (bf16[256,12,64]{0,2,1:T(8,128)(2,1)}, bf16[256,12,64]{0,2,1:T(8,128)(2,1)}, u32[]{:S(2)}, u32[]{:S(2)}) collective-permute-start(bf16[256,12,64]{0,2,1:T(8,128)(2,1)} %fusion.190), channel_id=1, source_target_pairs={{0,1},{1,2},{2,3},{3,4},{4,5},{5,6},{6,7},{7,0},{8,9},{9,10},{10,1... | collective-permute-start | bytes 1179656 | tf_op jit(solution)/shard_map/while/body/eval_jaxpr/ppermute | solution.py:15
  533.1 15.1 %collective-permute-start = (bf16[256,12,64]{0,2,1:T(8,128)(2,1)S(1)}, bf16[256,12,64]{0,2,1:T(8,128)(2,1)}, u32[]{:S(2)}, u32[]{:S(2)}) collective-permute-start(bf16[256,12,64]{0,2,1:T(8,128)(2,1)S(1)} %copy.76), channel_id=1, source_target_pairs={{0,1},{1,2},{2,3},{3,4},{4,5},{5,6},{6,7},{7,0},{8,9},{9,10},{10,1... | collective-permute-start | bytes 1179656 | tf_op jit(solution)/shard_map/while/body/eval_jaxpr/ppermute | solution.py:15
  533.1 19.3 %collective-permute-start.1 = (bf16[256,12,64]{0,2,1:T(8,128)(2,1)}, bf16[256,12,64]{0,2,1:T(8,128)(2,1)}, u32[]{:S(2)}, u32[]{:S(2)}) collective-permute-start(bf16[256,12,64]{0,2,1:T(8,128)(2,1)} %copy.77), channel_id=1, source_target_pairs={{0,1},{1,2},{2,3},{3,4},{4,5},{5,6},{6,7},{7,0},{8,9},{9,10},{10,1... | collective-permute-start | bytes 1179656 | tf_op jit(solution)/shard_map/while/body/eval_jaxpr/ppermute | solution.py:15
  559.5 133.5 %all-reduce.20.cloned.1.call-start = ((), (), s32[]{:S(2)}) async-start(), calls=%async_computation.14 | async-start | bytes 7077888 | tf_op jit(solution)/shard_map/psum | solution.py:292
  569.9 71.1 %copy-start.11 = (bf16[256,3072]{1,0:T(8,128)(2,1)S(1)}, bf16[256,3072]{1,0:T(8,128)(2,1)}, u32[]{:S(2)}) copy-start(bf16[256,3072]{1,0:T(8,128)(2,1)} %copy-done.10) | copy-start | bytes 4718596
  (80 other events, 467.7 us)
Sparse Core Ops, SparseCore 0:
  9.9 50.0 all-gather.9
  68.5 39.1 all-gather.11
  109.9 39.1 all-gather.19
  150.8 55.2 all-gather.15
  207.8 57.0 all-gather.17
  266.6 27.7 all-gather.13
  297.3 28.5 reduce-scatter.6
  328.8 57.0 reduce-scatter.8
  388.9 57.0 reduce-scatter.10
  559.6 44.8 reduce-scatter.4
  607.1 85.8 all-reduce.19
where the time goes:
time: 711 us; the launch traced here: 707 us
  waiting for transfers between devices  329 us (46%)
  matrix products  151 us (21%)
  blocking collectives  69.9 us (10%)
  other arithmetic  63.4 us (9%)
  local copies, waits for them, and re-layouts  62.1 us (9%)
  between operations  17.8 us (3%)
  loops' own time  8.68 us (1%)
    ppermute x32, waiting for transfers between devices, from_behind(): return lax.ppermute(x, axis, [(i, (i + by) % size) for i in range(size)])  113 us
    psum x1, waiting for transfers between devices, on_device(): lax.psum(shares[0].astype(jnp.bfloat16), 'ctx').astype(jnp.float32)  45.3 us
    all_gather x1, waiting for transfers between devices, on_device(): value_piece = lax.all_gather(values, 'ctx', axis=0, tiled=True)  41.4 us
    all_gather x1, waiting for transfers between devices, on_device(): lax.all_gather(down_weight, 'fsdp', axis=0, tiled=True)  38.2 us
    reduce_scatter x1, waiting for transfers between devices, on_device(): lax.psum_scatter(in_weight_part.astype(jnp.bfloat16), 'fsdp', scatter_dim...  34.4 us
    unnamed x2, blocking collectives  33.7 us
    while x108, local copies, waits for them, and re-layouts  31 us
    all_gather x1, waiting for transfers between devices, on_device(): lax.all_gather(in_weight, 'fsdp', axis=0, tiled=True)  22.8 us
  transfers between devices with their start and end apart: 43, of which 39 were waited for; matrix products, arithmetic and copies ran while one was open for 35% of the time, Pallas kernels for 0%

commit v1 on v0

--- a/solution.py
+++ b/solution.py
@@ -8,6 +8,17 @@
 ROT = 16
 NEG = -1e30
 EPS = 1e-05
+
+
+def turned_line(shard, name, dim):
+    count = lax.axis_size(name)
+    right = [(i, (i + 1) % count) for i in range(count)]
+    parts = [shard]
+    for hop in range(1, count):
+        parts = [lax.ppermute(parts[0], name, right), *parts]
+    result = jnp.concatenate(parts, axis=dim)
+    shift = (lax.axis_index(name) + 1) * parts[-1].shape[dim]
+    return jnp.roll(result, shift, axis=dim)
 
 
 def from_behind(x, axis, by):
@@ -169,7 +180,7 @@
     )
     carry = start_state
     key_piece = lax.all_gather(keys, "ctx", axis=0, tiled=True)
-    value_piece = lax.all_gather(values, "ctx", axis=0, tiled=True)
+    value_piece = turned_line(values, "ctx", 0)
     count = key_piece.shape[0]
     size = 512
 

time: 711 us -> 680 us (0.956)
  waiting for transfers between devices: 329 us -> 289 us
    ppermute x0 -> x7, waiting for transfers between devices: none -> 70.3 us  [turned_line(): parts = [lax.ppermute(parts[0], name, right), *parts]]
    all_gather x1 -> x0, waiting for transfers between devices: 41.4 us -> none  [on_device(): value_piece = lax.all_gather(values, 'ctx', axis=0, tiled=True)]
    all_gather x1, waiting for transfers between devices: 38.2 us -> 0.02 us  [on_device(): lax.all_gather(down_weight, 'fsdp', axis=0, tiled=True)]
    all_gather x1, waiting for transfers between devices: 17.6 us -> 0.02 us  [on_device(): lax.all_gather(out_weight, 'fsdp', axis=0, tiled=True)]
    all_gather x1, waiting for transfers between devices: 13.7 us -> 0.01 us  [on_device(): key_piece = lax.all_gather(keys, 'ctx', axis=0, tiled=True)]
    unnamed x106 -> x143, local copies, waits for them, and re-layouts: 11.4 us -> 18.6 us
  transfers between devices with their start and end apart: 43 -> 49, of which waited for: 39 -> 41; matrix products, arithmetic and copies ran while one was open for 35% -> 38% of each run, Pallas kernels for 0% -> 0%
where the time goes in v1:
time: 680 us; the launch traced here: 676 us
  waiting for transfers between devices  289 us (42%)
  matrix products  153 us (22%)
  local copies, waits for them, and re-layouts  69 us (10%)
  other arithmetic  67.2 us (10%)
  blocking collectives  66.9 us (10%)
  between operations  18.4 us (3%)
  loops' own time  8.7 us (1%)
    ppermute x32, waiting for transfers between devices, from_behind(): return lax.ppermute(x, axis, [(i, (i + by) % size) for i in range(size)])  114 us
    ppermute x7, waiting for transfers between devices, turned_line(): parts = [lax.ppermute(parts[0], name, right), *parts]  70.3 us
    psum x1, waiting for transfers between devices, on_device(): lax.psum(shares[0].astype(jnp.bfloat16), 'ctx').astype(jnp.float32)  45.1 us
    reduce_scatter x1, waiting for transfers between devices, on_device(): lax.psum_scatter(in_weight_part.astype(jnp.bfloat16), 'fsdp', scatter_dim...  34.4 us
    unnamed x2, blocking collectives  33.7 us
    while x108, local copies, waits for them, and re-layouts  30.5 us
    all_gather x1, waiting for transfers between devices, on_device(): lax.all_gather(in_weight, 'fsdp', axis=0, tiled=True)  22.8 us
    dot_general x4, matrix products, softmax_step(): jnp.einsum('qhd,khd->hqk', queries, keys, preferred_element_type=jnp.floa...  22 us
  transfers between devices with their start and end apart: 49, of which 41 were waited for; matrix products, arithmetic and copies ran while one was open for 38% of the time, Pallas kernels for 0%

profile of v1, /device:TPU:0, one launch (start us, length us, event | category | flops | bytes accessed | tf_op | source)
XLA Modules:
  0.0 675.8 jit_solution(13908686526716915741)
XLA Ops:
  14.8 18.4 %all-reduce.17 = (bf16[768]{0:T(1024)(128)(2,1)}, bf16[768]{0:T(1024)(128)(2,1)}, bf16[2304]{0:T(1024)(128)(2,1)S(1)}, bf16[768]{0:T(1024)(128)(2,1)S(1)}, bf16[768]{0:T(1024)(128)(2,1)S(1)}) all-reduce(bf16[768]{0:T(1024)(128)(2,1)S(1)} %dynamic-update-slice.5, ...), channel_id=1, replica_groups=mesh['fsdp'=4,'ctx'=8] {'fsdp'}, use_global_device_ids=true, to_apply=%add.5 | all-reduce | flops 5376 | bytes 21504
  37.1 22.8 %all-gather.8.cloned.1.call-done = bf16[768,2304]{1,0:T(8,128)(2,1)} async-done(((bf16[192,2304]{1,0:T(8,128)(2,1)}), bf16[768,2304]{1,0:T(8,128)(2,1)}) %all-gather.8.cloned.1.call-update) | async-done | bytes 3538960 | tf_op jit(solution)/shard_map/all_gather | solution.py:120
  59.9 4.7 convolution_add_fusion
  70.7 9.3 %collective-permute-done.4 = bf16[256,12,64]{0,2,1:T(8,128)(2,1)S(1)} collective-permute-done((bf16[256,12,64]{0,2,1:T(8,128)(2,1)}, bf16[256,12,64]{0,2,1:T(8,128)(2,1)S(1)}, u32[]{:S(2)}, u32[]{:S(2)}) %collective-permute-start.4) | collective-permute-done | bytes 393248 | tf_op jit(solution)/shard_map/ppermute | solution.py:18
  80.0 17.3 %collective-permute-done.5 = bf16[256,12,64]{0,2,1:T(8,128)(2,1)S(1)} collective-permute-done((bf16[256,12,64]{0,2,1:T(8,128)(2,1)S(1)}, bf16[256,12,64]{0,2,1:T(8,128)(2,1)S(1)}, u32[]{:S(2)}, u32[]{:S(2)}) %collective-permute-start.5) | collective-permute-done | bytes 393248 | tf_op jit(solution)/shard_map/ppermute | solution.py:18
  98.0 16.6 %collective-permute-done.6 = bf16[256,12,64]{0,2,1:T(8,128)(2,1)S(1)} collective-permute-done((bf16[256,12,64]{0,2,1:T(8,128)(2,1)S(1)}, bf16[256,12,64]{0,2,1:T(8,128)(2,1)S(1)}, u32[]{:S(2)}, u32[]{:S(2)}) %collective-permute-start.6) | collective-permute-done | bytes 393248 | tf_op jit(solution)/shard_map/ppermute | solution.py:18
  115.3 9.0 %collective-permute-done.7 = bf16[256,12,64]{0,2,1:T(8,128)(2,1)S(1)} collective-permute-done((bf16[256,12,64]{0,2,1:T(8,128)(2,1)S(1)}, bf16[256,12,64]{0,2,1:T(8,128)(2,1)S(1)}, u32[]{:S(2)}, u32[]{:S(2)}) %collective-permute-start.7) | collective-permute-done | bytes 393248 | tf_op jit(solution)/shard_map/ppermute | solution.py:18
  125.1 9.0 %collective-permute-done.8 = bf16[256,12,64]{0,2,1:T(8,128)(2,1)S(1)} collective-permute-done((bf16[256,12,64]{0,2,1:T(8,128)(2,1)S(1)}, bf16[256,12,64]{0,2,1:T(8,128)(2,1)S(1)}, u32[]{:S(2)}, u32[]{:S(2)}) %collective-permute-start.8) | collective-permute-done | bytes 393248 | tf_op jit(solution)/shard_map/ppermute | solution.py:18
  134.8 9.1 %collective-permute-done.9 = bf16[256,12,64]{0,2,1:T(8,128)(2,1)} collective-permute-done((bf16[256,12,64]{0,2,1:T(8,128)(2,1)S(1)}, bf16[256,12,64]{0,2,1:T(8,128)(2,1)}, u32[]{:S(2)}, u32[]{:S(2)}) %collective-permute-start.9) | collective-permute-done | bytes 393248 | tf_op jit(solution)/shard_map/ppermute | solution.py:18
  147.2 8.2 %all-gather.1 = bf16[4,1,768]{2,1,0:T(2,128)(2,1)S(1)} all-gather(bf16[1,1,768]{2,1,0:T(2,128)(2,1)S(1)} %reshape.292), channel_id=1, replica_groups=mesh['fsdp'=4,'ctx'=8] {'fsdp'}, dimensions={0}, use_global_device_ids=true | all-gather | bytes 7680 | tf_op jit(solution)/shard_map/all_gather | solution.py:125
  156.1 9.6 %all-gather = s32[1,2048]{1,0:T(1,128)} all-gather(s32[1,256]{1,0:T(1,128)} %param.20), channel_id=2, replica_groups=mesh['fsdp'=4,'ctx'=8] {'ctx'}, dimensions={1}, use_global_device_ids=true | all-gather | bytes 9216 | tf_op jit(solution)/shard_map/all_gather | solution.py:152
  174.3 64.2 %while.39 = (s32[]{:T(128)}, f32[12,256]{1,0:T(8,128)S(1)}, f32[12,256]{1,0:T(8,128)S(1)}, f32[256,12,64]{0,2,1:T(8,128)S(1)}, s32[4]{0:T(128)S(1)}, /*index=5*/...) while((s32[]{:T(128)}, f32[12,256]{1,0:T(8,128)S(1)}, ...), condition=%wide.region_5.6_spmd.clone, body=%wide.region_2.5_spmd.clone.sunk | while | flops 420694016 | bytes 48307420 | solution.py:194
  178.5 5.5 fusion.174
  184.0 5.6 fusion.178
  195.2 5.5 fusion.174
  200.8 4.8 fusion.178
  211.1 5.5 fusion.174
  216.6 4.8 fusion.178
  226.9 5.5 fusion.174
  232.4 4.7 fusion.178
  240.6 11.4 %multiply_convert_fusion.1 = (bf16[256,3072]{1,0:T(8,128)(2,1)S(1)}, f32[256,3072]{1,0:T(8,128)}, f32[256,3072]{1,0:T(8,128)}) fusion(f32[3072]{0:T(1024)S(1)} %bitcast.236, bf16[768,3072]{1,0:T(8,128)(2,1)} %all-gather.14.cloned.1.call-done, bf16[1,256,768]{2,1,0:T(8,128)(2,1)S(1)} %copy-done.3, f32[768]{0:T(1024)S(1)} %copy-done.40, ...), kind=kOutput, calls=%fused_computation.54 | convolution fusion | flops 1261043712 | bytes 12996608 | tf_op jit(solution)/shard_map/dot_general | solution.py:199
  252.0 7.6 %fusion.120 = (bf16[3072]{0:T(1024)(128)(2,1)}, bf16[256,3072]{1,0:T(8,128)(2,1)S(1)}) fusion(f32[256,3072]{1,0:T(8,128)} %get-tuple-element.561, f32[256,3072]{1,0:T(8,128)} %get-tuple-element.585, bf16[3072,768]{1,0:T(8,128)(2,1)} %all-gather.16.cloned.1.call-done, bf16[1,256,768]{2,1,0:T(8,128)(2,1)S(1)} %copy-done.4), kind=kOutput, calls=%fused_computation.190 | convolution fusion | flops 1219752960 | bytes 12982272 | tf_op jit(solution)/shard_map/dot_general | solution.py:58
  260.7 3.7 convolution_convert_fusion.1
  269.0 3.6 convolution_convert_fusion
  276.0 245.1 %while.40 = (s32[]{:T(128)}, bf16[256,12,64]{0,2,1:T(8,128)(2,1)}, bf16[256,12,64]{0,2,1:T(8,128)(2,1)}, f32[256,12,64]{0,2,1:T(8,128)S(1)}, f32[256,12,64]{0,2,...) while((s32[]{:T(128)}, bf16[256,12,64]{0,2,1:T(8,128)(2,1)}, ...), condition=%wide.region_9.10_spmd.clone, body=%wide.region_8.9_spmd.clone.sunk | while | flops 513605632 | bytes 40837772 | solution.py:251
  302.5 4.2 collective-permute-done.1
  320.4 4.4 collective-permute-done.2
  333.2 4.2 collective-permute-done.1
  350.3 5.0 collective-permute-done.2
  363.8 4.2 collective-permute-done.1
  380.9 5.0 collective-permute-done.2
  387.0 3.1 collective-permute-done.3
  394.4 4.2 collective-permute-done.1
  411.6 5.0 collective-permute-done.2
  425.1 4.2 collective-permute-done.1
  442.2 5.0 collective-permute-done.2
  455.7 4.2 collective-permute-done.1
  472.8 5.0 collective-permute-done.2
  486.3 4.2 collective-permute-done.1
  503.4 5.0 collective-permute-done.2
  516.9 4.2 collective-permute-done.1
  524.9 3.2 convolution_convert_fusion.2
  531.6 4.8 fusion.122
  538.7 34.4 %reduce-scatter.5.cloned.1.call-done = bf16[192,2304]{1,0:T(8,128)(2,1)} async-done(((bf16[768,2304]{1,0:T(8,128)(2,1)}), bf16[192,2304]{1,0:T(8,128)(2,1)}) %reduce-scatter.5.cloned.1.call-update) | async-done | bytes 884752 | tf_op jit(solution)/shard_map/reduce_scatter | solution.py:268
  575.1 15.3 %all-reduce.16 = (bf16[768]{0:T(1024)(128)(2,1)S(1)}, bf16[768]{0:T(1024)(128)(2,1)S(1)}, bf16[2304]{0:T(1024)(128)(2,1)S(1)}, bf16[768]{0:T(1024)(128)(2,1)S(1)...) all-reduce(bf16[768]{0:T(1024)(128)(2,1)S(1)} %dynamic-update-slice, ...), channel_id=1, replica_groups=mesh['fsdp'=4,'ctx'=8] {'fsdp'}, use_global_device_ids=true, to_apply=%add.6 | all-reduce | flops 10752 | bytes 43008
  591.0 15.3 %all-reduce.14 = (bf16[576]{0:T(1024)(128)(2,1)S(1)}, bf16[192]{0:T(256)(128)(2,1)S(1)}, bf16[768]{0:T(1024)(128)(2,1)S(1)}, bf16[192]{0:T(256)(128)(2,1)S(1)}, ...) all-reduce(bf16[576]{0:T(1024)(128)(2,1)S(1)} %dynamic-slice.8, ...), channel_id=1, replica_groups=mesh['fsdp'=4,'ctx'=8] {'ctx'}, use_global_device_ids=true, to_apply=%region_16.17 | all-reduce | flops 2304 | bytes 9216 | tf_op jit(solution)/shard_map/psum | solution.py:304
  609.8 3.9 convolution_add_fusion.3
  616.4 45.1 %all-reduce.20.cloned.1.call-done = (bf16[192,2304]{1,0:T(8,128)(2,1)}, bf16[192,768]{1,0:T(8,128)(2,1)}, bf16[192,3072]{1,0:T(8,128)(2,1)}, bf16[768,768]{1,0:T(8,128)(2,1)}) async-done(((bf16[192,2304]{1,0:T(8,128)(2,1)}, bf16[192,768]{1,0:T(8,128)(2,1)}, bf16[192,3072]{1,0:T(8,128)(2,1)}, bf16[768,768]{1,0:T(8,128)(2,1)}), (bf16[192,2304]{1,0:T(8,128)(2,1)}, bf16[192,768]{1,0:T(8,128)(2,1)}, ...) | async-done | bytes 3538960 | tf_op jit(solution)/shard_map/psum | solution.py:303
  (499 shorter events, 252.9 us)
Async XLA Ops:
  7.2 52.8 %all-gather.8.cloned.1.call-start = ((), (), s32[]{:S(2)}) async-start(), calls=%async_computation.4 | async-start | bytes 4423680 | tf_op jit(solution)/shard_map/all_gather | solution.py:120
  7.9 166.4 %all-gather.10.cloned.1.call-start = ((), (), s32[]{:S(2)}) async-start(), calls=%async_computation.5 | async-start | bytes 3538944 | tf_op jit(solution)/shard_map/all_gather | solution.py:182
  68.5 172.0 %all-gather.14.cloned.1.call-start = ((), (), s32[]{:S(2)}) async-start(), calls=%async_computation.7 | async-start | bytes 5898240 | tf_op jit(solution)/shard_map/all_gather | solution.py:124
  69.2 182.7 %all-gather.16.cloned.1.call-start = ((), (), s32[]{:S(2)}) async-start(), calls=%async_computation.8 | async-start | bytes 5898240 | tf_op jit(solution)/shard_map/all_gather | solution.py:126
  69.8 194.8 %all-gather.12.cloned.1.call-start = ((), (), s32[]{:S(2)}) async-start(), calls=%async_computation.6 | async-start | bytes 1474560 | tf_op jit(solution)/shard_map/all_gather | solution.py:122
  70.7 9.3 %collective-permute-start.4 = (bf16[256,12,64]{0,2,1:T(8,128)(2,1)}, bf16[256,12,64]{0,2,1:T(8,128)(2,1)S(1)}, u32[]{:S(2)}, u32[]{:S(2)}) collective-permute-start(bf16[256,12,64]{0,2,1:T(8,128)(2,1)} %fusion.81), channel_id=1, source_target_pairs={{0,1},{1,2},{2,3},{3,4},{4,5},{5,6},{6,7},{7,0},{8,9},{9,10},{10,1... | collective-permute-start | bytes 1179656 | tf_op jit(solution)/shard_map/ppermute | solution.py:18
  80.0 17.3 %collective-permute-start.5 = (bf16[256,12,64]{0,2,1:T(8,128)(2,1)S(1)}, bf16[256,12,64]{0,2,1:T(8,128)(2,1)S(1)}, u32[]{:S(2)}, u32[]{:S(2)}) collective-permute-start(bf16[256,12,64]{0,2,1:T(8,128)(2,1)S(1)} %collective-permute-done.4), channel_id=1, source_target_pairs={{0,1},{1,2},{2,3},{3,4},{4,5},{5,6},{6,7},{7,0},{8,9},{9,10},{10,1... | collective-permute-start | bytes 1179656 | tf_op jit(solution)/shard_map/ppermute | solution.py:18
  98.0 16.6 %collective-permute-start.6 = (bf16[256,12,64]{0,2,1:T(8,128)(2,1)S(1)}, bf16[256,12,64]{0,2,1:T(8,128)(2,1)S(1)}, u32[]{:S(2)}, u32[]{:S(2)}) collective-permute-start(bf16[256,12,64]{0,2,1:T(8,128)(2,1)S(1)} %collective-permute-done.5), channel_id=1, source_target_pairs={{0,1},{1,2},{2,3},{3,4},{4,5},{5,6},{6,7},{7,0},{8,9},{9,10},{10,1... | collective-permute-start | bytes 1179656 | tf_op jit(solution)/shard_map/ppermute | solution.py:18
  115.3 9.0 %collective-permute-start.7 = (bf16[256,12,64]{0,2,1:T(8,128)(2,1)S(1)}, bf16[256,12,64]{0,2,1:T(8,128)(2,1)S(1)}, u32[]{:S(2)}, u32[]{:S(2)}) collective-permute-start(bf16[256,12,64]{0,2,1:T(8,128)(2,1)S(1)} %collective-permute-done.6), channel_id=1, source_target_pairs={{0,1},{1,2},{2,3},{3,4},{4,5},{5,6},{6,7},{7,0},{8,9},{9,10},{10,1... | collective-permute-start | bytes 1179656 | tf_op jit(solution)/shard_map/ppermute | solution.py:18
  134.8 9.1 %collective-permute-start.9 = (bf16[256,12,64]{0,2,1:T(8,128)(2,1)S(1)}, bf16[256,12,64]{0,2,1:T(8,128)(2,1)}, u32[]{:S(2)}, u32[]{:S(2)}) collective-permute-start(bf16[256,12,64]{0,2,1:T(8,128)(2,1)S(1)} %collective-permute-done.8), channel_id=1, source_target_pairs={{0,1},{1,2},{2,3},{3,4},{4,5},{5,6},{6,7},{7,0},{8,9},{9,10},{10,1... | collective-permute-start | bytes 1179656 | tf_op jit(solution)/shard_map/ppermute | solution.py:18
  143.9 23.3 %collective-permute-start.10 = (bf16[256,12,64]{0,2,1:T(8,128)(2,1)}, bf16[256,12,64]{0,2,1:T(8,128)(2,1)}, u32[]{:S(2)}, u32[]{:S(2)}) collective-permute-start(bf16[256,12,64]{0,2,1:T(8,128)(2,1)} %collective-permute-done.9), channel_id=1, source_target_pairs={{0,1},{1,2},{2,3},{3,4},{4,5},{5,6},{6,7},{7,0},{8,9},{9,10},{10,1... | collective-permute-start | bytes 1179656 | tf_op jit(solution)/shard_map/ppermute | solution.py:18
  144.0 394.7 %reduce-scatter.7.cloned.1.call-start = ((), (), s32[]{:S(2)}) async-start(), calls=%async_computation.10 | async-start | bytes 1474560 | tf_op jit(solution)/shard_map/reduce_scatter | solution.py:274
  240.2 298.4 %reduce-scatter.9.cloned.1.call-start = ((), (), s32[]{:S(2)}) async-start(), calls=%async_computation.11 | async-start | bytes 5898240 | tf_op jit(solution)/shard_map/reduce_scatter | solution.py:280
  264.5 274.2 %reduce-scatter.11.cloned.1.call-start = ((), (), s32[]{:S(2)}) async-start(), calls=%async_computation.12 | async-start | bytes 5898240 | tf_op jit(solution)/shard_map/reduce_scatter | solution.py:286
  272.6 300.5 %reduce-scatter.5.cloned.1.call-start = ((), (), s32[]{:S(2)}) async-start(), calls=%async_computation.9 | async-start | bytes 4423680 | tf_op jit(solution)/shard_map/reduce_scatter | solution.py:268
  284.7 9.3 %collective-permute-start.2 = (bf16[256,12,64]{0,2,1:T(8,128)(2,1)}, bf16[256,12,64]{0,2,1:T(8,128)(2,1)}, u32[]{:S(2)}, u32[]{:S(2)}) collective-permute-start(bf16[256,12,64]{0,2,1:T(8,128)(2,1)} %fusion.190), channel_id=1, source_target_pairs={{0,1},{1,2},{2,3},{3,4},{4,5},{5,6},{6,7},{7,0},{8,9},{9,10},{10,1... | collective-permute-start | bytes 1179656 | tf_op jit(solution)/shard_map/while/body/eval_jaxpr/ppermute | solution.py:26
  287.5 10.7 %collective-permute-start.3 = (bf16[256,12,64]{0,2,1:T(8,128)(2,1)}, bf16[256,12,64]{0,2,1:T(8,128)(2,1)}, u32[]{:S(2)}, u32[]{:S(2)}) collective-permute-start(bf16[256,12,64]{0,2,1:T(8,128)(2,1)} %fusion.191), channel_id=1, source_target_pairs={{0,1},{1,2},{2,3},{3,4},{4,5},{5,6},{6,7},{7,0},{8,9},{9,10},{10,1... | collective-permute-start | bytes 1179656 | tf_op jit(solution)/shard_map/while/body/eval_jaxpr/ppermute | solution.py:26
  288.7 13.8 %collective-permute-start = (bf16[256,12,64]{0,2,1:T(8,128)(2,1)S(1)}, bf16[256,12,64]{0,2,1:T(8,128)(2,1)}, u32[]{:S(2)}, u32[]{:S(2)}) collective-permute-start(bf16[256,12,64]{0,2,1:T(8,128)(2,1)S(1)} %copy.91), channel_id=1, source_target_pairs={{0,1},{1,2},{2,3},{3,4},{4,5},{5,6},{6,7},{7,0},{8,9},{9,10},{10,1... | collective-permute-start | bytes 1179656 | tf_op jit(solution)/shard_map/while/body/eval_jaxpr/ppermute | solution.py:26
  288.9 17.7 %collective-permute-start.1 = (bf16[256,12,64]{0,2,1:T(8,128)(2,1)}, bf16[256,12,64]{0,2,1:T(8,128)(2,1)}, u32[]{:S(2)}, u32[]{:S(2)}) collective-permute-start(bf16[256,12,64]{0,2,1:T(8,128)(2,1)} %copy.92), channel_id=1, source_target_pairs={{0,1},{1,2},{2,3},{3,4},{4,5},{5,6},{6,7},{7,0},{8,9},{9,10},{10,1... | collective-permute-start | bytes 1179656 | tf_op jit(solution)/shard_map/while/body/eval_jaxpr/ppermute | solution.py:26
  315.4 9.3 %collective-permute-start.2 = (bf16[256,12,64]{0,2,1:T(8,128)(2,1)}, bf16[256,12,64]{0,2,1:T(8,128)(2,1)}, u32[]{:S(2)}, u32[]{:S(2)}) collective-permute-start(bf16[256,12,64]{0,2,1:T(8,128)(2,1)} %fusion.190), channel_id=1, source_target_pairs={{0,1},{1,2},{2,3},{3,4},{4,5},{5,6},{6,7},{7,0},{8,9},{9,10},{10,1... | collective-permute-start | bytes 1179656 | tf_op jit(solution)/shard_map/while/body/eval_jaxpr/ppermute | solution.py:26
  318.1 10.9 %collective-permute-start.3 = (bf16[256,12,64]{0,2,1:T(8,128)(2,1)}, bf16[256,12,64]{0,2,1:T(8,128)(2,1)}, u32[]{:S(2)}, u32[]{:S(2)}) collective-permute-start(bf16[256,12,64]{0,2,1:T(8,128)(2,1)} %fusion.191), channel_id=1, source_target_pairs={{0,1},{1,2},{2,3},{3,4},{4,5},{5,6},{6,7},{7,0},{8,9},{9,10},{10,1... | collective-permute-start | bytes 1179656 | tf_op jit(solution)/shard_map/while/body/eval_jaxpr/ppermute | solution.py:26
  318.1 15.1 %collective-permute-start = (bf16[256,12,64]{0,2,1:T(8,128)(2,1)S(1)}, bf16[256,12,64]{0,2,1:T(8,128)(2,1)}, u32[]{:S(2)}, u32[]{:S(2)}) collective-permute-start(bf16[256,12,64]{0,2,1:T(8,128)(2,1)S(1)} %copy.91), channel_id=1, source_target_pairs={{0,1},{1,2},{2,3},{3,4},{4,5},{5,6},{6,7},{7,0},{8,9},{9,10},{10,1... | collective-permute-start | bytes 1179656 | tf_op jit(solution)/shard_map/while/body/eval_jaxpr/ppermute | solution.py:26
  318.1 19.3 %collective-permute-start.1 = (bf16[256,12,64]{0,2,1:T(8,128)(2,1)}, bf16[256,12,64]{0,2,1:T(8,128)(2,1)}, u32[]{:S(2)}, u32[]{:S(2)}) collective-permute-start(bf16[256,12,64]{0,2,1:T(8,128)(2,1)} %copy.92), channel_id=1, source_target_pairs={{0,1},{1,2},{2,3},{3,4},{4,5},{5,6},{6,7},{7,0},{8,9},{9,10},{10,1... | collective-permute-start | bytes 1179656 | tf_op jit(solution)/shard_map/while/body/eval_jaxpr/ppermute | solution.py:26
  346.0 9.3 %collective-permute-start.2 = (bf16[256,12,64]{0,2,1:T(8,128)(2,1)}, bf16[256,12,64]{0,2,1:T(8,128)(2,1)}, u32[]{:S(2)}, u32[]{:S(2)}) collective-permute-start(bf16[256,12,64]{0,2,1:T(8,128)(2,1)} %fusion.190), channel_id=1, source_target_pairs={{0,1},{1,2},{2,3},{3,4},{4,5},{5,6},{6,7},{7,0},{8,9},{9,10},{10,1... | collective-permute-start | bytes 1179656 | tf_op jit(solution)/shard_map/while/body/eval_jaxpr/ppermute | solution.py:26
  348.7 10.9 %collective-permute-start.3 = (bf16[256,12,64]{0,2,1:T(8,128)(2,1)}, bf16[256,12,64]{0,2,1:T(8,128)(2,1)}, u32[]{:S(2)}, u32[]{:S(2)}) collective-permute-start(bf16[256,12,64]{0,2,1:T(8,128)(2,1)} %fusion.191), channel_id=1, source_target_pairs={{0,1},{1,2},{2,3},{3,4},{4,5},{5,6},{6,7},{7,0},{8,9},{9,10},{10,1... | collective-permute-start | bytes 1179656 | tf_op jit(solution)/shard_map/while/body/eval_jaxpr/ppermute | solution.py:26
  348.7 15.1 %collective-permute-start = (bf16[256,12,64]{0,2,1:T(8,128)(2,1)S(1)}, bf16[256,12,64]{0,2,1:T(8,128)(2,1)}, u32[]{:S(2)}, u32[]{:S(2)}) collective-permute-start(bf16[256,12,64]{0,2,1:T(8,128)(2,1)S(1)} %copy.91), channel_id=1, source_target_pairs={{0,1},{1,2},{2,3},{3,4},{4,5},{5,6},{6,7},{7,0},{8,9},{9,10},{10,1... | collective-permute-start | bytes 1179656 | tf_op jit(solution)/shard_map/while/body/eval_jaxpr/ppermute | solution.py:26
  348.7 19.3 %collective-permute-start.1 = (bf16[256,12,64]{0,2,1:T(8,128)(2,1)}, bf16[256,12,64]{0,2,1:T(8,128)(2,1)}, u32[]{:S(2)}, u32[]{:S(2)}) collective-permute-start(bf16[256,12,64]{0,2,1:T(8,128)(2,1)} %copy.92), channel_id=1, source_target_pairs={{0,1},{1,2},{2,3},{3,4},{4,5},{5,6},{6,7},{7,0},{8,9},{9,10},{10,1... | collective-permute-start | bytes 1179656 | tf_op jit(solution)/shard_map/while/body/eval_jaxpr/ppermute | solution.py:26
  376.6 9.3 %collective-permute-start.2 = (bf16[256,12,64]{0,2,1:T(8,128)(2,1)}, bf16[256,12,64]{0,2,1:T(8,128)(2,1)}, u32[]{:S(2)}, u32[]{:S(2)}) collective-permute-start(bf16[256,12,64]{0,2,1:T(8,128)(2,1)} %fusion.190), channel_id=1, source_target_pairs={{0,1},{1,2},{2,3},{3,4},{4,5},{5,6},{6,7},{7,0},{8,9},{9,10},{10,1... | collective-permute-start | bytes 1179656 | tf_op jit(solution)/shard_map/while/body/eval_jaxpr/ppermute | solution.py:26
  379.3 10.9 %collective-permute-start.3 = (bf16[256,12,64]{0,2,1:T(8,128)(2,1)}, bf16[256,12,64]{0,2,1:T(8,128)(2,1)}, u32[]{:S(2)}, u32[]{:S(2)}) collective-permute-start(bf16[256,12,64]{0,2,1:T(8,128)(2,1)} %fusion.191), channel_id=1, source_target_pairs={{0,1},{1,2},{2,3},{3,4},{4,5},{5,6},{6,7},{7,0},{8,9},{9,10},{10,1... | collective-permute-start | bytes 1179656 | tf_op jit(solution)/shard_map/while/body/eval_jaxpr/ppermute | solution.py:26
  379.3 15.1 %collective-permute-start = (bf16[256,12,64]{0,2,1:T(8,128)(2,1)S(1)}, bf16[256,12,64]{0,2,1:T(8,128)(2,1)}, u32[]{:S(2)}, u32[]{:S(2)}) collective-permute-start(bf16[256,12,64]{0,2,1:T(8,128)(2,1)S(1)} %copy.91), channel_id=1, source_target_pairs={{0,1},{1,2},{2,3},{3,4},{4,5},{5,6},{6,7},{7,0},{8,9},{9,10},{10,1... | collective-permute-start | bytes 1179656 | tf_op jit(solution)/shard_map/while/body/eval_jaxpr/ppermute | solution.py:26
  379.3 19.3 %collective-permute-start.1 = (bf16[256,12,64]{0,2,1:T(8,128)(2,1)}, bf16[256,12,64]{0,2,1:T(8,128)(2,1)}, u32[]{:S(2)}, u32[]{:S(2)}) collective-permute-start(bf16[256,12,64]{0,2,1:T(8,128)(2,1)} %copy.92), channel_id=1, source_target_pairs={{0,1},{1,2},{2,3},{3,4},{4,5},{5,6},{6,7},{7,0},{8,9},{9,10},{10,1... | collective-permute-start | bytes 1179656 | tf_op jit(solution)/shard_map/while/body/eval_jaxpr/ppermute | solution.py:26
  407.3 9.3 %collective-permute-start.2 = (bf16[256,12,64]{0,2,1:T(8,128)(2,1)}, bf16[256,12,64]{0,2,1:T(8,128)(2,1)}, u32[]{:S(2)}, u32[]{:S(2)}) collective-permute-start(bf16[256,12,64]{0,2,1:T(8,128)(2,1)} %fusion.190), channel_id=1, source_target_pairs={{0,1},{1,2},{2,3},{3,4},{4,5},{5,6},{6,7},{7,0},{8,9},{9,10},{10,1... | collective-permute-start | bytes 1179656 | tf_op jit(solution)/shard_map/while/body/eval_jaxpr/ppermute | solution.py:26
  410.0 10.9 %collective-permute-start.3 = (bf16[256,12,64]{0,2,1:T(8,128)(2,1)}, bf16[256,12,64]{0,2,1:T(8,128)(2,1)}, u32[]{:S(2)}, u32[]{:S(2)}) collective-permute-start(bf16[256,12,64]{0,2,1:T(8,128)(2,1)} %fusion.191), channel_id=1, source_target_pairs={{0,1},{1,2},{2,3},{3,4},{4,5},{5,6},{6,7},{7,0},{8,9},{9,10},{10,1... | collective-permute-start | bytes 1179656 | tf_op jit(solution)/shard_map/while/body/eval_jaxpr/ppermute | solution.py:26
  410.0 15.1 %collective-permute-start = (bf16[256,12,64]{0,2,1:T(8,128)(2,1)S(1)}, bf16[256,12,64]{0,2,1:T(8,128)(2,1)}, u32[]{:S(2)}, u32[]{:S(2)}) collective-permute-start(bf16[256,12,64]{0,2,1:T(8,128)(2,1)S(1)} %copy.91), channel_id=1, source_target_pairs={{0,1},{1,2},{2,3},{3,4},{4,5},{5,6},{6,7},{7,0},{8,9},{9,10},{10,1... | collective-permute-start | bytes 1179656 | tf_op jit(solution)/shard_map/while/body/eval_jaxpr/ppermute | solution.py:26
  410.0 19.3 %collective-permute-start.1 = (bf16[256,12,64]{0,2,1:T(8,128)(2,1)}, bf16[256,12,64]{0,2,1:T(8,128)(2,1)}, u32[]{:S(2)}, u32[]{:S(2)}) collective-permute-start(bf16[256,12,64]{0,2,1:T(8,128)(2,1)} %copy.92), channel_id=1, source_target_pairs={{0,1},{1,2},{2,3},{3,4},{4,5},{5,6},{6,7},{7,0},{8,9},{9,10},{10,1... | collective-permute-start | bytes 1179656 | tf_op jit(solution)/shard_map/while/body/eval_jaxpr/ppermute | solution.py:26
  437.9 9.3 %collective-permute-start.2 = (bf16[256,12,64]{0,2,1:T(8,128)(2,1)}, bf16[256,12,64]{0,2,1:T(8,128)(2,1)}, u32[]{:S(2)}, u32[]{:S(2)}) collective-permute-start(bf16[256,12,64]{0,2,1:T(8,128)(2,1)} %fusion.190), channel_id=1, source_target_pairs={{0,1},{1,2},{2,3},{3,4},{4,5},{5,6},{6,7},{7,0},{8,9},{9,10},{10,1... | collective-permute-start | bytes 1179656 | tf_op jit(solution)/shard_map/while/body/eval_jaxpr/ppermute | solution.py:26
  440.6 10.9 %collective-permute-start.3 = (bf16[256,12,64]{0,2,1:T(8,128)(2,1)}, bf16[256,12,64]{0,2,1:T(8,128)(2,1)}, u32[]{:S(2)}, u32[]{:S(2)}) collective-permute-start(bf16[256,12,64]{0,2,1:T(8,128)(2,1)} %fusion.191), channel_id=1, source_target_pairs={{0,1},{1,2},{2,3},{3,4},{4,5},{5,6},{6,7},{7,0},{8,9},{9,10},{10,1... | collective-permute-start | bytes 1179656 | tf_op jit(solution)/shard_map/while/body/eval_jaxpr/ppermute | solution.py:26
  440.6 15.1 %collective-permute-start = (bf16[256,12,64]{0,2,1:T(8,128)(2,1)S(1)}, bf16[256,12,64]{0,2,1:T(8,128)(2,1)}, u32[]{:S(2)}, u32[]{:S(2)}) collective-permute-start(bf16[256,12,64]{0,2,1:T(8,128)(2,1)S(1)} %copy.91), channel_id=1, source_target_pairs={{0,1},{1,2},{2,3},{3,4},{4,5},{5,6},{6,7},{7,0},{8,9},{9,10},{10,1... | collective-permute-start | bytes 1179656 | tf_op jit(solution)/shard_map/while/body/eval_jaxpr/ppermute | solution.py:26
  440.6 19.3 %collective-permute-start.1 = (bf16[256,12,64]{0,2,1:T(8,128)(2,1)}, bf16[256,12,64]{0,2,1:T(8,128)(2,1)}, u32[]{:S(2)}, u32[]{:S(2)}) collective-permute-start(bf16[256,12,64]{0,2,1:T(8,128)(2,1)} %copy.92), channel_id=1, source_target_pairs={{0,1},{1,2},{2,3},{3,4},{4,5},{5,6},{6,7},{7,0},{8,9},{9,10},{10,1... | collective-permute-start | bytes 1179656 | tf_op jit(solution)/shard_map/while/body/eval_jaxpr/ppermute | solution.py:26
  468.6 9.3 %collective-permute-start.2 = (bf16[256,12,64]{0,2,1:T(8,128)(2,1)}, bf16[256,12,64]{0,2,1:T(8,128)(2,1)}, u32[]{:S(2)}, u32[]{:S(2)}) collective-permute-start(bf16[256,12,64]{0,2,1:T(8,128)(2,1)} %fusion.190), channel_id=1, source_target_pairs={{0,1},{1,2},{2,3},{3,4},{4,5},{5,6},{6,7},{7,0},{8,9},{9,10},{10,1... | collective-permute-start | bytes 1179656 | tf_op jit(solution)/shard_map/while/body/eval_jaxpr/ppermute | solution.py:26
  471.2 10.9 %collective-permute-start.3 = (bf16[256,12,64]{0,2,1:T(8,128)(2,1)}, bf16[256,12,64]{0,2,1:T(8,128)(2,1)}, u32[]{:S(2)}, u32[]{:S(2)}) collective-permute-start(bf16[256,12,64]{0,2,1:T(8,128)(2,1)} %fusion.191), channel_id=1, source_target_pairs={{0,1},{1,2},{2,3},{3,4},{4,5},{5,6},{6,7},{7,0},{8,9},{9,10},{10,1... | collective-permute-start | bytes 1179656 | tf_op jit(solution)/shard_map/while/body/eval_jaxpr/ppermute | solution.py:26
  471.2 15.1 %collective-permute-start = (bf16[256,12,64]{0,2,1:T(8,128)(2,1)S(1)}, bf16[256,12,64]{0,2,1:T(8,128)(2,1)}, u32[]{:S(2)}, u32[]{:S(2)}) collective-permute-start(bf16[256,12,64]{0,2,1:T(8,128)(2,1)S(1)} %copy.91), channel_id=1, source_target_pairs={{0,1},{1,2},{2,3},{3,4},{4,5},{5,6},{6,7},{7,0},{8,9},{9,10},{10,1... | collective-permute-start | bytes 1179656 | tf_op jit(solution)/shard_map/while/body/eval_jaxpr/ppermute | solution.py:26
  471.2 19.3 %collective-permute-start.1 = (bf16[256,12,64]{0,2,1:T(8,128)(2,1)}, bf16[256,12,64]{0,2,1:T(8,128)(2,1)}, u32[]{:S(2)}, u32[]{:S(2)}) collective-permute-start(bf16[256,12,64]{0,2,1:T(8,128)(2,1)} %copy.92), channel_id=1, source_target_pairs={{0,1},{1,2},{2,3},{3,4},{4,5},{5,6},{6,7},{7,0},{8,9},{9,10},{10,1... | collective-permute-start | bytes 1179656 | tf_op jit(solution)/shard_map/while/body/eval_jaxpr/ppermute | solution.py:26
  499.2 9.3 %collective-permute-start.2 = (bf16[256,12,64]{0,2,1:T(8,128)(2,1)}, bf16[256,12,64]{0,2,1:T(8,128)(2,1)}, u32[]{:S(2)}, u32[]{:S(2)}) collective-permute-start(bf16[256,12,64]{0,2,1:T(8,128)(2,1)} %fusion.190), channel_id=1, source_target_pairs={{0,1},{1,2},{2,3},{3,4},{4,5},{5,6},{6,7},{7,0},{8,9},{9,10},{10,1... | collective-permute-start | bytes 1179656 | tf_op jit(solution)/shard_map/while/body/eval_jaxpr/ppermute | solution.py:26
  501.8 10.9 %collective-permute-start.3 = (bf16[256,12,64]{0,2,1:T(8,128)(2,1)}, bf16[256,12,64]{0,2,1:T(8,128)(2,1)}, u32[]{:S(2)}, u32[]{:S(2)}) collective-permute-start(bf16[256,12,64]{0,2,1:T(8,128)(2,1)} %fusion.191), channel_id=1, source_target_pairs={{0,1},{1,2},{2,3},{3,4},{4,5},{5,6},{6,7},{7,0},{8,9},{9,10},{10,1... | collective-permute-start | bytes 1179656 | tf_op jit(solution)/shard_map/while/body/eval_jaxpr/ppermute | solution.py:26
  501.8 15.1 %collective-permute-start = (bf16[256,12,64]{0,2,1:T(8,128)(2,1)S(1)}, bf16[256,12,64]{0,2,1:T(8,128)(2,1)}, u32[]{:S(2)}, u32[]{:S(2)}) collective-permute-start(bf16[256,12,64]{0,2,1:T(8,128)(2,1)S(1)} %copy.91), channel_id=1, source_target_pairs={{0,1},{1,2},{2,3},{3,4},{4,5},{5,6},{6,7},{7,0},{8,9},{9,10},{10,1... | collective-permute-start | bytes 1179656 | tf_op jit(solution)/shard_map/while/body/eval_jaxpr/ppermute | solution.py:26
  501.8 19.3 %collective-permute-start.1 = (bf16[256,12,64]{0,2,1:T(8,128)(2,1)}, bf16[256,12,64]{0,2,1:T(8,128)(2,1)}, u32[]{:S(2)}, u32[]{:S(2)}) collective-permute-start(bf16[256,12,64]{0,2,1:T(8,128)(2,1)} %copy.92), channel_id=1, source_target_pairs={{0,1},{1,2},{2,3},{3,4},{4,5},{5,6},{6,7},{7,0},{8,9},{9,10},{10,1... | collective-permute-start | bytes 1179656 | tf_op jit(solution)/shard_map/while/body/eval_jaxpr/ppermute | solution.py:26
  528.1 133.4 %all-reduce.20.cloned.1.call-start = ((), (), s32[]{:S(2)}) async-start(), calls=%async_computation.13 | async-start | bytes 7077888 | tf_op jit(solution)/shard_map/psum | solution.py:303
  (97 other events, 941.6 us)
Sparse Core Ops, SparseCore 0:
  9.9 50.0 all-gather.7
  68.6 47.2 all-gather.9
  117.8 57.7 all-gather.13
  177.2 57.1 all-gather.15
  236.1 27.7 all-gather.11
  267.2 28.5 reduce-scatter.6
  298.8 57.0 reduce-scatter.8
  358.9 57.0 reduce-scatter.10
  528.3 44.8 reduce-scatter.4
  575.6 85.8 all-reduce.19
